TPU v7x, 32 devices: a whole 2x2x4 slice. The times are simulated.
32 devices in a mesh: groups: 2 (over y), ctx: 4 (over z), head: 2 (over x), rows: 2 (over core).
Axes of the slice: x: 2, y: 2, z: 4, core: 2. Of those that a mesh axis runs over, the one named last changes fastest.
Arguments:
- keys: bfloat16 [65536, 1024], P(('groups', 'ctx'), 'head'), parts along dimension 0, may hold values from -18 to 18
- values: bfloat16 [65536, 1024], P(('groups', 'ctx'), 'head'), parts along dimension 0, may hold values from -6 to 6
- window_q: bfloat16 [64, 8192], P(('groups', 'ctx'), 'head'), parts along dimension 0, may hold values from -6 to 6
- keep_stretches: int32 [16, 20], P(('groups', 'head')), parts along dimension 0, may hold values from 0 to 62, as said below
- dec_q: bfloat16 [128, 4, 8192], P('groups', None, 'head'), parts along dimension 0, may hold values from -6 to 6
- dec_k: bfloat16 [128, 4, 1024], P('groups', None, 'head'), parts along dimension 0, may hold values from -8 to 8
- dec_v: bfloat16 [128, 4, 1024], P('groups', None, 'head'), parts along dimension 0, may hold values from -6 to 6
- row_order: int32 [128], P('groups'), parts along dimension 0, may hold values from 0 to 63, each once
Outputs:
- stretch_scores: float32 [16, 64], P(('groups', 'head', 'rows'), 'ctx'), parts along dimension 0
- decoded: bfloat16 [128, 4, 8192], P(('groups', 'ctx', 'rows'), None, 'head'), parts along dimension 0
There are 2 independent parts, one for each index of `groups`. A program takes and returns all parts, laid end to end along the dimension named above; each array names one. Nothing has to cross between parts.
Inputs may be any that keep to these rules, and one draw needn't show every extreme that they name: keep_stretches[k] lists 20 distinct stretch numbers of key-value head k in ascending order and never the last stretch; for every head some context shard has all 16 of its stretches listed.
All inputs are finite; a program needn't handle non-finite values.
Results may differ from a plain program's by a relative error of at most 0.0045.
Values may be sent and summed in bfloat16 or wider, within the bound.
A program may use at most 128 MiB of HBM per device.

v0:
```python
import functools
import math

import jax
import jax.numpy as jnp
from jax import lax
from jax.experimental import pallas as pl
from jax.experimental.pallas import tpu as pltpu
from jax.sharding import PartitionSpec as P

QH = 64
KVH = 8
HD = 128
STRETCH = 512
W = 32
FILL = -1e30
SCALE = HD ** -0.5 * math.log2(math.e)
NT = (((1,), (1,)), ((), ()))
TN = (((0,), (0,)), ((), ()))
VMEM_LIMIT = 48 * 1024 * 1024


def dot(a, b, dims):
    return lax.dot_general(a, b, dims, preferred_element_type=jnp.float32)


def decode_kernel(parts, steps, meta, keep, pick, dq, dk, dv, k_ref, v_ref, out, lse, q_s, acc, m_s, l_s):
    head = pl.program_id(0)
    group = dq.shape[1] // HD
    per = pick.shape[0] // parts
    cols = group * per
    stretches = k_ref.shape[0] // STRETCH
    base = meta[0] * stretches

    gathered = dot(pick[...], dq[...], (((1,), (0,)), ((), ()))).astype(jnp.bfloat16)
    for d in range(parts):
        for g in range(group):
            q_s[pl.ds(d * cols + g * per, per), :] = gathered[d * per:(d + 1) * per, g * HD:(g + 1) * HD]
    acc[...] = jnp.zeros_like(acc)
    m_s[...] = jnp.full_like(m_s, FILL)
    l_s[...] = jnp.zeros_like(l_s)

    def update(key, value, mask=None):
        for d in range(parts):
            at = pl.ds(d * cols, cols)
            s = dot(key, q_s[at, :], NT)
            if mask is not None:
                s = jnp.where(mask(d, s.shape), s, FILL)
            m_old = m_s[:, at]
            m_new = jnp.maximum(m_old, jnp.max(s, axis=0, keepdims=True))
            p = jnp.exp2(s * SCALE - m_new * SCALE)
            shrink = jnp.exp2((m_old - m_new) * SCALE)
            m_s[:, at] = m_new
            l_s[:, at] = l_s[:, at] * shrink + jnp.sum(p, axis=0, keepdims=True)
            acc[:, at] = acc[:, at] * shrink + dot(value, p.astype(jnp.bfloat16), TN)

    def count(i, found):
        start, many = found
        stretch = keep[head, i] - base
        return (start + (stretch < 0).astype(jnp.int32),
                many + ((stretch >= 0) & (stretch < stretches)).astype(jnp.int32))

    start, many = lax.fori_loop(0, keep.shape[1], count, (jnp.int32(0), jnp.int32(0)))

    def one(i, carry):
        at = pl.ds(pl.multiple_of((keep[head, start + i] - base) * STRETCH, STRETCH), STRETCH)
        update(k_ref[at, :], v_ref[at, :])
        return carry

    lax.fori_loop(0, many, one, 0)

    @pl.when(meta[1] == 1)
    def _():
        tail = pl.ds(k_ref.shape[0] - W, W)
        update(k_ref[tail, :], v_ref[tail, :])
        own_k = dot(pick[...], dk[...], (((1,), (0,)), ((), ()))).astype(jnp.bfloat16)
        own_v = dot(pick[...], dv[...], (((1,), (0,)), ((), ()))).astype(jnp.bfloat16)
        each = per // steps

        def mask(d, shape):
            key_at = lax.broadcasted_iota(jnp.int32, shape, 0)
            query_at = lax.broadcasted_iota(jnp.int32, shape, 1) % per
            inside = key_at % per
            return ((key_at // per == d) & (inside % each == query_at % each)
                    & (inside // each <= query_at // each))

        update(own_k, own_v, mask)

    l = l_s[...]
    some = l > 0.0
    safe = jnp.where(some, l, 1.0)
    inverse = jnp.where(some, 1.0 / safe, 0.0)
    level = jnp.where(some, m_s[...] * SCALE + jnp.log2(safe), FILL)
    for d in range(parts):
        at = pl.ds(d * cols, cols)
        out[d] = (acc[:, at] * inverse[:, d * cols:(d + 1) * cols]).astype(jnp.bfloat16)
        lse[d] = level[:, d * cols:(d + 1) * cols]


def decode(meta, keep, pick, dq, dk, dv, keys, values, parts, steps):
    heads = keys.shape[1] // HD
    group = dq.shape[1] // (heads * HD)
    count = pick.shape[0] * group
    cols = count // parts
    ctx = keys.shape[0]
    column = lambda rows, width: pl.BlockSpec((rows, width), lambda h, *_: (0, h))
    return pl.pallas_call(
        functools.partial(decode_kernel, parts, steps),
        grid_spec=pltpu.PrefetchScalarGridSpec(
            num_scalar_prefetch=2,
            grid=(heads,),
            in_specs=[
                pl.BlockSpec(pick.shape, lambda h, *_: (0, 0)),
                column(dq.shape[0], group * HD),
                column(dk.shape[0], HD),
                column(dv.shape[0], HD),
                column(ctx, HD),
                column(ctx, HD),
            ],
            out_specs=[
                pl.BlockSpec((parts, None, HD, cols), lambda h, *_: (0, h, 0, 0)),
                pl.BlockSpec((parts, None, 1, cols), lambda h, *_: (0, h, 0, 0)),
            ],
            scratch_shapes=[
                pltpu.VMEM((count, HD), jnp.bfloat16),
                pltpu.VMEM((HD, count), jnp.float32),
                pltpu.VMEM((1, count), jnp.float32),
                pltpu.VMEM((1, count), jnp.float32),
            ],
        ),
        out_shape=[
            jax.ShapeDtypeStruct((parts, heads, HD, cols), jnp.bfloat16),
            jax.ShapeDtypeStruct((parts, heads, 1, cols), jnp.float32),
        ],
        compiler_params=pltpu.CompilerParams(vmem_limit_bytes=VMEM_LIMIT),
        name="decode",
    )(meta, keep, pick, dq, dk, dv, keys, values)


def window_kernel(meta, q_ref, k_ref, out, q_s):
    group = q_ref.shape[1] // HD
    for g in range(group):
        q_s[pl.ds(g * W, W), :] = q_ref[:, pl.ds(g * HD, HD)]
    stretches = k_ref.shape[0] // STRETCH

    def level(c, masked):
        s = dot(k_ref[pl.ds(pl.multiple_of(c * STRETCH, STRETCH), STRETCH), :], q_s[...], NT)
        if masked:
            key_at = lax.broadcasted_iota(jnp.int32, s.shape, 0)
            query_at = lax.broadcasted_iota(jnp.int32, s.shape, 1) % W
            s = jnp.where((key_at <= STRETCH - W + query_at) | (meta[1] == 0), s, FILL)
        m = jnp.max(s, axis=0, keepdims=True)
        total = jnp.sum(jnp.exp2(s * SCALE - m * SCALE), axis=0, keepdims=True)
        out[pl.ds(c, 1), :] = m * SCALE + jnp.log2(total)

    def one(c, carry):
        level(c, False)
        return carry

    lax.fori_loop(0, stretches - 1, one, 0)
    level(stretches - 1, True)


def window(meta, queries, keys, heads):
    width = queries.shape[1] // heads
    stretches = keys.shape[0] // STRETCH
    count = W * (width // HD)
    return pl.pallas_call(
        window_kernel,
        grid_spec=pltpu.PrefetchScalarGridSpec(
            num_scalar_prefetch=1,
            grid=(heads,),
            in_specs=[
                pl.BlockSpec((W, width), lambda h, meta: (0, h)),
                pl.BlockSpec((keys.shape[0], HD), lambda h, meta: (0, meta[2] + h)),
            ],
            out_specs=pl.BlockSpec((None, stretches, count), lambda h, meta: (h, 0, 0)),
            scratch_shapes=[pltpu.VMEM((count, HD), jnp.bfloat16)],
        ),
        out_shape=jax.ShapeDtypeStruct((heads, stretches, count), jnp.float32),
        compiler_params=pltpu.CompilerParams(vmem_limit_bytes=VMEM_LIMIT),
        name="window",
    )(meta, queries, keys)


def combine_kernel(part, lse, out):
    parts = part.shape[0]
    top = lse[0]
    for i in range(1, parts):
        top = jnp.maximum(top, lse[i])
    total = jnp.zeros_like(top)
    summed = jnp.zeros(part.shape[1:], jnp.float32)
    for i in range(parts):
        share = jnp.exp2(lse[i] - top)
        total = total + share
        summed = summed + part[i].astype(jnp.float32) * share
    turned = (summed / total).T.astype(jnp.bfloat16)
    per = out.shape[0]
    for g in range(turned.shape[0] // per):
        out[:, pl.ds(g * HD, HD)] = turned[g * per:(g + 1) * per, :]


def combine(part, lse, per):
    parts, heads, depth, cols = part.shape
    width = cols // per * HD
    return pl.pallas_call(
        combine_kernel,
        grid=(heads,),
        in_specs=[
            pl.BlockSpec((parts, None, depth, cols), lambda h: (0, h, 0, 0)),
            pl.BlockSpec((parts, None, 1, cols), lambda h: (0, h, 0, 0)),
        ],
        out_specs=pl.BlockSpec((per, width), lambda h: (0, h)),
        out_shape=jax.ShapeDtypeStruct((per, heads * width), jnp.bfloat16),
        name="combine",
    )(part, lse)


def local(keys, values, window_q, keep_stretches, dec_q, dec_k, dec_v, row_order):
    parts = lax.axis_size("ctx")
    row_count = lax.axis_size("rows")
    own = lax.axis_index("ctx")
    row = lax.axis_index("rows")
    heads = keys.shape[1] // HD
    score_heads = heads // row_count
    rows, steps, _ = dec_q.shape
    each = rows // (parts * row_count)
    meta = jnp.stack([own, (own == parts - 1).astype(jnp.int32), row * score_heads]).astype(jnp.int32)

    cols = window_q.shape[1] // row_count
    mine = lax.dynamic_slice_in_dim(window_q, row * cols, cols, 1)
    queries = lax.all_gather(mine, "ctx", axis=0, tiled=True)

    order = lax.dynamic_slice_in_dim(row_order.reshape(parts, row_count, each), row, 1, 1)
    wanted = order * steps + jnp.arange(steps, dtype=jnp.int32)[None, :, None]
    pick = (wanted.reshape(-1)[:, None] == jnp.arange(rows * steps, dtype=jnp.int32)[None, :])
    pick = pick.astype(jnp.bfloat16)

    flat = lambda x: x.reshape(rows * steps, x.shape[2])
    part, lse = decode(meta, keep_stretches, pick, flat(dec_q), flat(dec_k), flat(dec_v), keys, values, parts, steps)
    part = lax.all_to_all(part, "ctx", 0, 0, tiled=True)
    lse = lax.all_to_all(lse, "ctx", 0, 0, tiled=True)

    level = window(meta, queries, keys, score_heads)
    top = jnp.max(level, axis=1)
    lower = jnp.log2(jnp.sum(jnp.exp2(level - top[:, None, :]), axis=1)) + top
    everyone = lax.all_gather(lower, "ctx")
    top = jnp.max(everyone, axis=0)
    whole = jnp.log2(jnp.sum(jnp.exp2(everyone - top), axis=0)) + top
    stretch_scores = jnp.sum(jnp.exp2(level - whole[:, None, :]), axis=2)

    decoded = combine(part, lse, steps * each)
    decoded = decoded.reshape(steps, each, -1).transpose(1, 0, 2)
    return stretch_scores, decoded


def solution(mesh):
    placed = (
        P(("groups", "ctx"), "head"),
        P(("groups", "ctx"), "head"),
        P(("groups", "ctx"), "head"),
        P(("groups", "head"), None),
        P("groups", None, "head"),
        P("groups", None, "head"),
        P("groups", None, "head"),
        P("groups"),
    )
    return jax.shard_map(
        local,
        mesh=mesh,
        in_specs=placed,
        out_specs=(
            P(("groups", "head", "rows"), "ctx"),
            P(("groups", "ctx", "rows"), None, "head"),
        ),
        check_vma=False,
    )
```

profile of v0, /device:TPU:6, one launch (start us, length us, event | category | flops | bytes accessed | tf_op | source)
XLA Modules:
  0.0 185.9 jit_solution(13100989829303974531)
XLA Ops:
  0.6 0.0 copy-start
  0.7 0.8 reshape.63
  1.4 0.1 add.57
  1.5 0.1 fusion.pick
  1.6 1.0 reshape.65.dk
  2.7 1.0 reshape.66.dv
  3.7 2.5 %reshape.64.dq = bf16[256,4096]{1,0:T(8,128)(2,1)S(1)} reshape(bf16[64,4,4096]{2,1,0:T(4,128)(2,1)} %param.12) | data formatting | bytes 4194304 | tf_op jit(solution)/shard_map/reshape | solution.py:239
  6.2 0.1 pad_add_fusion.meta
  6.3 0.0 copy-start.2
  6.3 0.7 copy-done.2
  7.0 18.0 %decode.1 = (bf16[4,4,128,256]{3,2,1,0:T(8,128)(2,1)S(1)}, f32[4,4,1,256]{3,2,1,0:T(1,128)S(1)}) custom-call(s32[3]{0:T(128)S(1)} %pad_add_fusion.meta, s32[4,20]{1,0:T(4,128)S(1)} %copy-done.2, bf16[128,256]{1,0:T(8,128)(2,1)S(1)} %fusion.pick, bf16[256,4096]{1,0:T(8,128)(2,1)S(1)} %reshape.64.dq, bf16[256,512]{1,0:T(8,128)(2,1)S(1)} %reshape.65.dk, ...), custom_call_target="tpu_custom_call" | custom-call | tf_op jit(solution)/shard_map/decode/pallas_call | solution.py:107
  25.1 0.0 copy-start.1
  25.1 1.0 copy-done.1
  26.0 92.7 %all_to_all.10.lse = f32[4,4,1,256]{3,2,1,0:T(1,128)} all-to-all(f32[4,4,1,256]{3,2,1,0:T(1,128)S(1)} %get-tuple-element.5), channel_id=1, replica_groups=mesh['groups'=2,'ctx'=4,'head'=2,'rows'=2] {'ctx'}, dimensions={0} | all-to-all | bytes 32768 | tf_op jit(solution)/shard_map/all_to_all | solution.py:242
  118.8 3.5 %all-to-all-start = ((bf16[4,4,128,256]{3,2,1,0:T(8,128)(2,1)}), bf16[4,4,128,256]{3,2,1,0:T(8,128)(2,1)S(1)}, u32[]{:S(2)}, u32[]{:S(2)}) async-start(bf16[4,4,128,256]{3,2,1,0:T(8,128)(2,1)} %copy-done.1), calls=%async_computation | async-start | bytes 2097152 | tf_op jit(solution)/shard_map/all_to_all | solution.py:241
  122.3 0.0 copy-done
  122.3 30.9 %all_gather.7.q_ref = bf16[32,2048]{1,0:T(8,128)(2,1)S(1)} all-gather(bf16[8,2048]{1,0:T(8,128)(2,1)S(1)} %constant_dynamic-slice_fusion), channel_id=1, replica_groups=mesh['groups'=2,'ctx'=4,'head'=2,'rows'=2] {'ctx'}, dimensions={0}, use_global_device_ids=true | all-gather | bytes 163840 | tf_op jit(solution)/shard_map/all_gather | solution.py:232
  153.2 13.7 %window.1 = f32[2,16,256]{2,1,0:T(8,128)S(1)} custom-call(s32[3]{0:T(128)S(1)} %pad_add_fusion.meta, bf16[32,2048]{1,0:T(8,128)(2,1)S(1)} %all_gather.7.q_ref, bf16[8192,512]{1,0:T(8,128)(2,1)} %k_ref.3), custom_call_target="tpu_custom_call" | custom-call | tf_op jit(solution)/shard_map/window/pallas_call | solution.py:168
  167.0 11.9 %all-gather.1 = f32[4,2,256]{2,1,0:T(2,128)S(1)} all-gather(f32[1,2,256]{2,1,0:T(2,128)S(1)} %add_bitcast_fusion), channel_id=2, replica_groups=mesh['groups'=2,'ctx'=4,'head'=2,'rows'=2] {'ctx'}, dimensions={0}, use_global_device_ids=true | all-gather | bytes 10240 | tf_op jit(solution)/shard_map/all_gather | solution.py:247
  178.9 0.7 exponential_reduce_fusion
  179.6 0.0 all-to-all-done.part
  179.6 0.0 copy-start.3
  179.6 1.0 copy-done.3
  180.6 3.5 %combine.1 = bf16[32,4096]{1,0:T(8,128)(2,1)} custom-call(bf16[4,4,128,256]{3,2,1,0:T(8,128)(2,1)} %copy-done.3, f32[4,4,1,256]{3,2,1,0:T(1,128)} %all_to_all.10.lse), custom_call_target="tpu_custom_call" | custom-call | tf_op jit(solution)/shard_map/combine/pallas_call | solution.py:206
  184.1 1.9 copy.13
  (9 shorter events, 0.1 us)
Async XLA Ops:
  0.6 121.7 %copy-start = (bf16[8,4096]{1,0:T(8,128)(2,1)S(1)}, bf16[8,4096]{1,0:T(8,128)(2,1)}, u32[]{:S(2)}) copy-start(bf16[8,4096]{1,0:T(8,128)(2,1)} %param.10) | copy-start | bytes 196612
  6.3 0.7 copy-start.2
  25.1 1.0 copy-start.1
  118.8 60.8 %all-to-all-start = ((bf16[4,4,128,256]{3,2,1,0:T(8,128)(2,1)}), bf16[4,4,128,256]{3,2,1,0:T(8,128)(2,1)S(1)}, u32[]{:S(2)}, u32[]{:S(2)}) async-start(bf16[4,4,128,256]{3,2,1,0:T(8,128)(2,1)} %copy-done.1), calls=%async_computation | async-start | bytes 2097152 | tf_op jit(solution)/shard_map/all_to_all | solution.py:241
  179.6 1.0 copy-start.3
where the time goes:
time: 186 us
  blocking collectives  135 us (73%)
  Pallas kernels  35.2 us (19%)
  local copies, waits for them, and re-layouts  9.97 us (5%)
  starting transfers between devices  3.52 us (2%)
    all_to_all x1, blocking collectives, local(): lse = lax.all_to_all(lse, 'ctx', 0, 0, tiled=True)  92.7 us
    all_gather x1, blocking collectives, local(): queries = lax.all_gather(mine, 'ctx', axis=0, tiled=True)  30.9 us
    pallas_call x1, Pallas kernels, decode(): pl.pallas_call(functools.partial(decode_kernel, parts, steps), grid_spec=...  18 us
    pallas_call x1, Pallas kernels, window(): pl.pallas_call(window_kernel, grid_spec=pltpu.PrefetchScalarGridSpec(num_...  13.7 us
    all_gather x1, blocking collectives, local(): everyone = lax.all_gather(lower, 'ctx')  11.9 us
    reshape x3, local copies, waits for them, and re-layouts, local(): flat = lambda x: x.reshape(rows * steps, x.shape[2])  4.58 us
  transfers between devices with their start and end apart: 1, of which 0 were waited for; matrix products, arithmetic and copies ran while one was open for 0% of the time, Pallas kernels for 7%

commit v1 on v0

v1 whole, which is shorter than its diff:
```python
import functools
import math

import jax
import jax.numpy as jnp
from jax import lax
from jax.experimental import pallas as pl
from jax.experimental.pallas import tpu as pltpu
from jax.sharding import PartitionSpec as P

QH = 64
KVH = 8
HD = 128
STRETCH = 512
W = 32
FILL = -1e30
SCALE = HD ** -0.5 * math.log2(math.e)
NN = (((1,), (0,)), ((), ()))
EXTRA = 16
UNROLL = 2
CHUNK = 512
VMEM_LIMIT = 48 * 1024 * 1024


def dot(a, b, dims):
    return lax.dot_general(a, b, dims, preferred_element_type=jnp.float32)


def decode_kernel(parts, steps, meta, keep, pick, dq, dk, dv, k_ref, v_ref, out, q_rows, q_s, acc, m_s, l_s):
    head = pl.program_id(0)
    group = dq.shape[1] // HD
    per = pick.shape[0] // parts
    cols = group * per
    stretches = k_ref.shape[0] // STRETCH
    base = meta[0] * stretches

    gathered = dot(pick[...], dq[...], NN)
    for d in range(parts):
        for g in range(group):
            q_rows[pl.ds(d * cols + g * per, per), :] = gathered[d * per:(d + 1) * per, g * HD:(g + 1) * HD]
    q_s[...] = q_rows[...].T.astype(jnp.bfloat16)
    acc[...] = jnp.zeros_like(acc)
    m_s[...] = jnp.full_like(m_s, FILL)
    l_s[...] = jnp.zeros_like(l_s)

    wide = math.gcd(CHUNK, parts * cols)
    chunks = parts * cols // wide

    def score(key, d):
        return dot(key, q_s[:, pl.ds(d * wide, wide)], NN)

    def fold(s, turned, d):
        at = pl.ds(d * wide, wide)
        m_old = m_s[:, at]
        m_new = jnp.maximum(m_old, jnp.max(s, axis=0, keepdims=True))
        p = jnp.exp2(s * SCALE - m_new * SCALE)
        shrink = jnp.exp2((m_old - m_new) * SCALE)
        both = dot(turned, p.astype(jnp.bfloat16), NN)
        m_s[:, at] = m_new
        l_s[:, at] = l_s[:, at] * shrink + both[HD:HD + 1]
        acc[:, at] = acc[:, at] * shrink + both[:HD]

    def update(blocks, mask=None):
        work = []
        for key, value in blocks:
            ones = jnp.ones((EXTRA, value.shape[0]), jnp.bfloat16)
            turned = jnp.concatenate([value.T, ones], axis=0)
            work += [(key, turned, d) for d in range(chunks)]
        later = score(work[0][0], work[0][2])
        for at, (_, turned, d) in enumerate(work):
            s = later
            if at + 1 < len(work):
                later = score(work[at + 1][0], work[at + 1][2])
            if mask is not None:
                s = jnp.where(mask(d, s.shape), s, FILL)
            fold(s, turned, d)

    def count(i, found):
        start, many = found
        stretch = keep[head, i] - base
        return (start + (stretch < 0).astype(jnp.int32),
                many + ((stretch >= 0) & (stretch < stretches)).astype(jnp.int32))

    start, many = lax.fori_loop(0, keep.shape[1], count, (jnp.int32(0), jnp.int32(0)))

    def block(i):
        at = pl.ds(pl.multiple_of((keep[head, start + i] - base) * STRETCH, STRETCH), STRETCH)
        return k_ref[at, :], v_ref[at, :]

    def several(i, carry):
        update([block(i * UNROLL + u) for u in range(UNROLL)])
        return carry

    def one(i, carry):
        update([block(i)])
        return carry

    lax.fori_loop(0, many // UNROLL, several, 0)
    lax.fori_loop(many // UNROLL * UNROLL, many, one, 0)

    @pl.when(meta[1] == 1)
    def _():
        tail = pl.ds(k_ref.shape[0] - W, W)
        update([(k_ref[tail, :], v_ref[tail, :])])
        own_k = dot(pick[...], dk[...], NN).astype(jnp.bfloat16)
        own_v = dot(pick[...], dv[...], NN).astype(jnp.bfloat16)
        each = per // steps

        def mask(d, shape):
            key_at = lax.broadcasted_iota(jnp.int32, shape, 0)
            query = lax.broadcasted_iota(jnp.int32, shape, 1) + d * wide
            query_at = query % per
            inside = key_at % per
            return ((key_at // per == query // cols) & (inside % each == query_at % each)
                    & (inside // each <= query_at // each))

        update([(own_k, own_v)], mask)

    l = l_s[...]
    some = l > 0.0
    safe = jnp.where(some, l, 1.0)
    inverse = jnp.where(some, 1.0 / safe, 0.0)
    level = jnp.where(some, m_s[...] * SCALE + jnp.log2(safe), FILL)
    high = level.astype(jnp.bfloat16).astype(jnp.float32)
    middle = (level - high).astype(jnp.bfloat16).astype(jnp.float32)
    low = level - high - middle
    pieces = jnp.concatenate([high, middle, low, jnp.zeros((EXTRA - 3, level.shape[1]), jnp.float32)], axis=0)
    for d in range(parts):
        at = pl.ds(d * cols, cols)
        out[d, :HD] = (acc[:, at] * inverse[:, d * cols:(d + 1) * cols]).astype(jnp.bfloat16)
        out[d, HD:] = pieces[:, d * cols:(d + 1) * cols].astype(jnp.bfloat16)


def decode(meta, keep, pick, dq, dk, dv, keys, values, parts, steps):
    heads = keys.shape[1] // HD
    group = dq.shape[1] // (heads * HD)
    count = pick.shape[0] * group
    cols = count // parts
    ctx = keys.shape[0]
    column = lambda rows, width: pl.BlockSpec((rows, width), lambda h, *_: (0, h))
    return pl.pallas_call(
        functools.partial(decode_kernel, parts, steps),
        grid_spec=pltpu.PrefetchScalarGridSpec(
            num_scalar_prefetch=2,
            grid=(heads,),
            in_specs=[
                pl.BlockSpec(pick.shape, lambda h, *_: (0, 0)),
                column(dq.shape[0], group * HD),
                column(dk.shape[0], HD),
                column(dv.shape[0], HD),
                column(ctx, HD),
                column(ctx, HD),
            ],
            out_specs=pl.BlockSpec((parts, None, HD + EXTRA, cols), lambda h, *_: (0, h, 0, 0)),
            scratch_shapes=[
                pltpu.VMEM((count, HD), jnp.float32),
                pltpu.VMEM((HD, count), jnp.bfloat16),
                pltpu.VMEM((HD, count), jnp.float32),
                pltpu.VMEM((1, count), jnp.float32),
                pltpu.VMEM((1, count), jnp.float32),
            ],
        ),
        out_shape=jax.ShapeDtypeStruct((parts, heads, HD + EXTRA, cols), jnp.bfloat16),
        cost_estimate=pl.CostEstimate(
            flops=2 * count * ctx * heads * HD, bytes_accessed=4 * ctx * heads * HD,
            transcendentals=count * ctx * heads // 2,
        ),
        compiler_params=pltpu.CompilerParams(vmem_limit_bytes=VMEM_LIMIT),
        name="decode",
    )(meta, keep, pick, dq, dk, dv, keys, values)


def window_kernel(meta, q_ref, k_ref, out, q_rows, q_s):
    group = q_ref.shape[1] // HD
    for g in range(group):
        q_rows[pl.ds(g * W, W), :] = q_ref[:, pl.ds(g * HD, HD)].astype(jnp.float32)
    q_s[...] = q_rows[...].T.astype(jnp.bfloat16)
    stretches = k_ref.shape[0] // STRETCH
    several = math.gcd(stretches, 4)

    def score(c):
        return dot(k_ref[pl.ds(pl.multiple_of(c * STRETCH, STRETCH), STRETCH), :], q_s[...], NN)

    def levels(first, last):
        later = score(first)
        for u in range(several):
            s = later
            if u + 1 < several:
                later = score(first + u + 1)
            if last and u + 1 == several:
                key_at = lax.broadcasted_iota(jnp.int32, s.shape, 0)
                query_at = lax.broadcasted_iota(jnp.int32, s.shape, 1) % W
                s = jnp.where((key_at <= STRETCH - W + query_at) | (meta[1] == 0), s, FILL)
            m = jnp.max(s, axis=0, keepdims=True)
            total = jnp.sum(jnp.exp2(s * SCALE - m * SCALE), axis=0, keepdims=True)
            out[pl.ds(first + u, 1), :] = m * SCALE + jnp.log2(total)

    def one(c, carry):
        levels(c * several, False)
        return carry

    lax.fori_loop(0, stretches // several - 1, one, 0)
    levels(stretches - several, True)


def window(meta, queries, keys, heads):
    width = queries.shape[1] // heads
    stretches = keys.shape[0] // STRETCH
    count = W * (width // HD)
    return pl.pallas_call(
        window_kernel,
        grid_spec=pltpu.PrefetchScalarGridSpec(
            num_scalar_prefetch=1,
            grid=(heads,),
            in_specs=[
                pl.BlockSpec((W, width), lambda h, meta: (0, h)),
                pl.BlockSpec((keys.shape[0], HD), lambda h, meta: (0, meta[2] + h)),
            ],
            out_specs=pl.BlockSpec((None, stretches, count), lambda h, meta: (h, 0, 0)),
            scratch_shapes=[pltpu.VMEM((count, HD), jnp.float32), pltpu.VMEM((HD, count), jnp.bfloat16)],
        ),
        out_shape=jax.ShapeDtypeStruct((heads, stretches, count), jnp.float32),
        compiler_params=pltpu.CompilerParams(vmem_limit_bytes=VMEM_LIMIT),
        name="window",
    )(meta, queries, keys)


def combine_kernel(part, out):
    parts = part.shape[0]
    blocks = [part[i].astype(jnp.float32) for i in range(parts)]
    levels = [b[HD:HD + 1] + b[HD + 1:HD + 2] + b[HD + 2:HD + 3] for b in blocks]
    top = levels[0]
    for level in levels[1:]:
        top = jnp.maximum(top, level)
    total = jnp.zeros_like(top)
    summed = jnp.zeros((HD, part.shape[2]), jnp.float32)
    for block, level in zip(blocks, levels):
        share = jnp.exp2(level - top)
        total = total + share
        summed = summed + block[:HD] * share
    turned = (summed / total).T.astype(jnp.bfloat16)
    per = out.shape[0]
    for g in range(turned.shape[0] // per):
        out[:, pl.ds(g * HD, HD)] = turned[g * per:(g + 1) * per, :]


def combine(part, per):
    parts, heads, depth, cols = part.shape
    width = cols // per * HD
    return pl.pallas_call(
        combine_kernel,
        grid=(heads,),
        in_specs=[pl.BlockSpec((parts, None, depth, cols), lambda h: (0, h, 0, 0))],
        out_specs=pl.BlockSpec((per, width), lambda h: (0, h)),
        out_shape=jax.ShapeDtypeStruct((per, heads * width), jnp.bfloat16),
        name="combine",
    )(part)


def others(x, axis):
    count = lax.axis_size(axis)
    return [lax.ppermute(x, axis, [(i, (i + shift) % count) for i in range(count)]) for shift in range(1, count)]


def local(keys, values, window_q, keep_stretches, dec_q, dec_k, dec_v, row_order):
    parts = lax.axis_size("ctx")
    row_count = lax.axis_size("rows")
    own = lax.axis_index("ctx")
    row = lax.axis_index("rows")
    heads = keys.shape[1] // HD
    score_heads = heads // row_count
    rows, steps, _ = dec_q.shape
    each = rows // (parts * row_count)
    meta = jnp.stack([own, (own == parts - 1).astype(jnp.int32), row * score_heads]).astype(jnp.int32)

    cols = window_q.shape[1] // row_count
    mine = lax.dynamic_slice_in_dim(window_q, row * cols, cols, 1)
    shifted = others(mine, "ctx")

    order = lax.dynamic_slice_in_dim(row_order.reshape(parts, row_count, each), row, 1, 1)
    wanted = order * steps + jnp.arange(steps, dtype=jnp.int32)[None, :, None]
    pick = (wanted.reshape(-1)[:, None] == jnp.arange(rows * steps, dtype=jnp.int32)[None, :])
    pick = pick.astype(jnp.bfloat16)

    queries = jnp.zeros((W, cols), mine.dtype)
    for shift, block in enumerate([mine] + shifted):
        at = lax.rem(own + parts - shift, parts) * mine.shape[0]
        queries = lax.dynamic_update_slice_in_dim(queries, block, at, 0)
    queries, pick = lax.optimization_barrier((queries, pick))

    flat = lambda x: x.reshape(rows * steps, x.shape[2])
    part = decode(meta, keep_stretches, pick, flat(dec_q), flat(dec_k), flat(dec_v), keys, values, parts, steps)
    part = lax.all_to_all(part, "ctx", 0, 0, tiled=True)

    level = window(meta, queries, keys, score_heads)
    top = jnp.max(level, axis=1)
    lower = jnp.log2(jnp.sum(jnp.exp2(level - top[:, None, :]), axis=1)) + top
    everyone = [lower] + others(lower, "ctx")
    top = functools.reduce(jnp.maximum, everyone)
    whole = jnp.log2(sum(jnp.exp2(one - top) for one in everyone)) + top
    stretch_scores = jnp.sum(jnp.exp2(level - whole[:, None, :]), axis=2)

    decoded = combine(part, steps * each)
    decoded = decoded.reshape(steps, each, -1).transpose(1, 0, 2)
    return stretch_scores, decoded


def solution(mesh):
    placed = (
        P(("groups", "ctx"), "head"),
        P(("groups", "ctx"), "head"),
        P(("groups", "ctx"), "head"),
        P(("groups", "head"), None),
        P("groups", None, "head"),
        P("groups", None, "head"),
        P("groups", None, "head"),
        P("groups"),
    )
    return jax.shard_map(
        local,
        mesh=mesh,
        in_specs=placed,
        out_specs=(
            P(("groups", "head", "rows"), "ctx"),
            P(("groups", "ctx", "rows"), None, "head"),
        ),
        check_vma=False,
    )
```

time: 186 us -> 102 us (0.55)
  the two profiles are of different devices: /device:TPU:6 before, /device:TPU:0 now
where the time goes in v1:
time: 102 us
  starting transfers between devices  52.8 us (52%)
  Pallas kernels  23.5 us (23%)
  waiting for transfers between devices  14.7 us (14%)
  local copies, waits for them, and re-layouts  9.1 us (9%)
    all_to_all x1, starting transfers between devices, local(): part = lax.all_to_all(part, 'ctx', 0, 0, tiled=True)  40 us
    ppermute x6, waiting for transfers between devices, others(): lax.ppermute(x, axis, [(i, (i + shift) % count) for i in range(count)])  14.7 us
    ppermute x6, starting transfers between devices, others(): lax.ppermute(x, axis, [(i, (i + shift) % count) for i in range(count)])  12.9 us
    pallas_call x1, Pallas kernels, decode(): pl.pallas_call(functools.partial(decode_kernel, parts, steps), grid_spec=...  11.7 us
    pallas_call x1, Pallas kernels, window(): pl.pallas_call(window_kernel, grid_spec=pltpu.PrefetchScalarGridSpec(num_...  8.34 us
    reshape x3, local copies, waits for them, and re-layouts, local(): flat = lambda x: x.reshape(rows * steps, x.shape[2])  4.58 us
    pallas_call x1, Pallas kernels, combine(): pl.pallas_call(combine_kernel, grid=(heads,), in_specs=[pl.BlockSpec((par...  3.48 us
  transfers between devices with their start and end apart: 7, of which 2 were waited for; matrix products, arithmetic and copies ran while one was open for 6% of the time, Pallas kernels for 8%

profile of v1, /device:TPU:0, one launch (start us, length us, event | category | flops | bytes accessed | tf_op | source)
XLA Modules:
  0.0 101.9 jit_solution(2206818594318390324)
XLA Ops:
  0.7 0.8 constant_dynamic-update-slice_fusion.3
  1.4 4.0 %collective-permute-start.1 = (bf16[8,2048]{1,0:T(8,128)(2,1)S(1)}, bf16[8,2048]{1,0:T(8,128)(2,1)S(1)}, u32[]{:S(2)}, u32[]{:S(2)}) collective-permute-start(bf16[8,2048]{1,0:T(8,128)(2,1)S(1)} %get-tuple-element.7), channel_id=1, source_target_pairs={{0,8},{4,12},{8,0},{12,4},{1,9},{5,13},{9,1},{13,5},{2,10},{6,14},... | collective-permute-start | bytes 98312 | tf_op jit(solution)/shard_map/ppermute | solution.py:262
  5.5 1.6 %collective-permute-start = (bf16[8,2048]{1,0:T(8,128)(2,1)S(1)}, bf16[8,2048]{1,0:T(8,128)(2,1)S(1)}, u32[]{:S(2)}, u32[]{:S(2)}) collective-permute-start(bf16[8,2048]{1,0:T(8,128)(2,1)S(1)} %get-tuple-element.7), channel_id=1, source_target_pairs={{0,4},{4,8},{8,12},{12,0},{1,5},{5,9},{9,13},{13,1},{2,6},{6,10},{... | collective-permute-start | bytes 98312 | tf_op jit(solution)/shard_map/ppermute | solution.py:262
  7.0 2.2 %collective-permute-start.2 = (bf16[8,2048]{1,0:T(8,128)(2,1)S(1)}, bf16[8,2048]{1,0:T(8,128)(2,1)S(1)}, u32[]{:S(2)}, u32[]{:S(2)}) collective-permute-start(bf16[8,2048]{1,0:T(8,128)(2,1)S(1)} %get-tuple-element.7), channel_id=1, source_target_pairs={{0,12},{4,0},{8,4},{12,8},{1,13},{5,1},{9,5},{13,9},{2,14},{6,2},{... | collective-permute-start | bytes 98312 | tf_op jit(solution)/shard_map/ppermute | solution.py:262
  9.3 0.7 reshape.35
  10.1 0.1 add.81
  10.2 0.1 fusion.pick
  10.2 0.1 pad_add_fusion.meta
  10.3 1.0 reshape.37.dk
  11.3 1.0 reshape.38.dv
  12.4 0.0 copy-start
  12.4 2.5 %reshape.36.dq = bf16[256,4096]{1,0:T(8,128)(2,1)S(1)} reshape(bf16[64,4,4096]{2,1,0:T(4,128)(2,1)} %param.12) | data formatting | bytes 4194304 | tf_op jit(solution)/shard_map/reshape | solution.py:291
  15.0 0.0 collective-permute-done
  15.0 0.0 collective-permute-done.1
  15.0 0.0 collective-permute-done.2
  15.0 0.0 copy-done
  15.0 11.7 %decode.1 = bf16[4,4,144,256]{3,2,1,0:T(8,128)(2,1)} custom-call(s32[3]{0:T(128)S(1)} %pad_add_fusion.meta, s32[4,20]{1,0:T(4,128)S(1)} %copy-done, bf16[128,256]{1,0:T(8,128)(2,1)S(1)} %fusion.pick, bf16[256,4096]{1,0:T(8,128)(2,1)S(1)} %reshape.36.dq, bf16[256,512]{1,0:T(8,128)(2,1)S(1)} %reshape.37.dk, bf16[256,512]{1,0:T(8,128)(2,1)S(1)} %reshape.38.dv, ...), custom_call_target="tpu_custom_call" | custom-call | flops 8589934592 | bytes 16777216 | tf_op jit(solution)/shard_map/decode/pallas_call | solution.py:141
  26.7 40.0 %all-to-all-start = ((bf16[4,4,144,256]{3,2,1,0:T(8,128)(2,1)}), bf16[4,4,144,256]{3,2,1,0:T(8,128)(2,1)S(1)}, u32[]{:S(2)}, u32[]{:S(2)}) async-start(bf16[4,4,144,256]{3,2,1,0:T(8,128)(2,1)} %decode.1), calls=%async_computation | async-start | bytes 2359296 | tf_op jit(solution)/shard_map/all_to_all | solution.py:293
  66.7 8.3 %window.1 = f32[2,16,256]{2,1,0:T(8,128)S(1)} custom-call(s32[3]{0:T(128)S(1)} %pad_add_fusion.meta, bf16[32,2048]{1,0:T(8,128)(2,1)S(1)} %constant_dynamic-update-slice_fusion.q_ref, bf16[8192,512]{1,0:T(8,128)(2,1)} %k_ref.3), custom_call_target="tpu_custom_call" | custom-call | tf_op jit(solution)/shard_map/window/pallas_call | solution.py:210
  75.2 3.9 %collective-permute-start.5 = (f32[2,256]{1,0:T(2,128)S(1)}, f32[2,256]{1,0:T(2,128)S(1)}, u32[]{:S(2)}, u32[]{:S(2)}) collective-permute-start(f32[2,256]{1,0:T(2,128)S(1)} %multiply_add_fusion.1), channel_id=1, source_target_pairs={{0,12},{4,0},{8,4},{12,8},{1,13},{5,1},{9,5},{13,9},{2,14},{6,2},{... | collective-permute-start | bytes 6152 | tf_op jit(solution)/shard_map/ppermute | solution.py:262
  79.0 0.0 collective-permute-start.4
  79.0 1.1 %collective-permute-start.3 = (f32[2,256]{1,0:T(2,128)S(1)}, f32[2,256]{1,0:T(2,128)S(1)}, u32[]{:S(2)}, u32[]{:S(2)}) collective-permute-start(f32[2,256]{1,0:T(2,128)S(1)} %multiply_add_fusion.1), channel_id=1, source_target_pairs={{0,4},{4,8},{8,12},{12,0},{1,5},{5,9},{9,13},{13,1},{2,6},{6,10},{... | collective-permute-start | bytes 6152 | tf_op jit(solution)/shard_map/ppermute | solution.py:262
  80.2 5.3 %collective-permute-done.5 = f32[2,256]{1,0:T(2,128)S(1)} collective-permute-done((f32[2,256]{1,0:T(2,128)S(1)}, f32[2,256]{1,0:T(2,128)S(1)}, u32[]{:S(2)}, u32[]{:S(2)}) %collective-permute-start.5) | collective-permute-done | bytes 2080 | tf_op jit(solution)/shard_map/ppermute | solution.py:262
  85.5 9.4 %collective-permute-done.4 = f32[2,256]{1,0:T(2,128)S(1)} collective-permute-done((f32[2,256]{1,0:T(2,128)S(1)}, f32[2,256]{1,0:T(2,128)S(1)}, u32[]{:S(2)}, u32[]{:S(2)}) %collective-permute-start.4) | collective-permute-done | bytes 2080 | tf_op jit(solution)/shard_map/ppermute | solution.py:262
  94.9 0.0 collective-permute-done.3
  94.9 0.7 exponential_reduce_fusion
  95.6 0.0 all-to-all-done.part
  95.6 0.0 copy-start.1
  95.6 1.0 copy-done.1
  96.6 3.5 %combine.1 = bf16[32,4096]{1,0:T(8,128)(2,1)} custom-call(bf16[4,4,144,256]{3,2,1,0:T(8,128)(2,1)} %copy-done.1), custom_call_target="tpu_custom_call" | custom-call | tf_op jit(solution)/shard_map/combine/pallas_call | solution.py:250
  100.1 1.9 %copy.12 = bf16[4,8,4096]{2,0,1:T(4,128)(2,1)} copy(bf16[4,8,4096]{2,1,0:T(8,128)(2,1)} %bitcast.8) | data formatting | bytes 524288 | tf_op jit(solution)/shard_map/reshape | solution.py:304
  (10 shorter events, 0.1 us)
Async XLA Ops:
  1.4 13.6 %collective-permute-start.1 = (bf16[8,2048]{1,0:T(8,128)(2,1)S(1)}, bf16[8,2048]{1,0:T(8,128)(2,1)S(1)}, u32[]{:S(2)}, u32[]{:S(2)}) collective-permute-start(bf16[8,2048]{1,0:T(8,128)(2,1)S(1)} %get-tuple-element.7), channel_id=1, source_target_pairs={{0,8},{4,12},{8,0},{12,4},{1,9},{5,13},{9,1},{13,5},{2,10},{6,14},... | collective-permute-start | bytes 98312 | tf_op jit(solution)/shard_map/ppermute | solution.py:262
  5.5 9.5 %collective-permute-start = (bf16[8,2048]{1,0:T(8,128)(2,1)S(1)}, bf16[8,2048]{1,0:T(8,128)(2,1)S(1)}, u32[]{:S(2)}, u32[]{:S(2)}) collective-permute-start(bf16[8,2048]{1,0:T(8,128)(2,1)S(1)} %get-tuple-element.7), channel_id=1, source_target_pairs={{0,4},{4,8},{8,12},{12,0},{1,5},{5,9},{9,13},{13,1},{2,6},{6,10},{... | collective-permute-start | bytes 98312 | tf_op jit(solution)/shard_map/ppermute | solution.py:262
  7.0 8.0 %collective-permute-start.2 = (bf16[8,2048]{1,0:T(8,128)(2,1)S(1)}, bf16[8,2048]{1,0:T(8,128)(2,1)S(1)}, u32[]{:S(2)}, u32[]{:S(2)}) collective-permute-start(bf16[8,2048]{1,0:T(8,128)(2,1)S(1)} %get-tuple-element.7), channel_id=1, source_target_pairs={{0,12},{4,0},{8,4},{12,8},{1,13},{5,1},{9,5},{13,9},{2,14},{6,2},{... | collective-permute-start | bytes 98312 | tf_op jit(solution)/shard_map/ppermute | solution.py:262
  12.4 2.7 %copy-start = (s32[4,20]{1,0:T(4,128)S(1)}, s32[4,20]{1,0:T(4,128)}, u32[]{:S(2)}) copy-start(s32[4,20]{1,0:T(4,128)} %keep.1) | copy-start | bytes 964
  26.7 68.8 %all-to-all-start = ((bf16[4,4,144,256]{3,2,1,0:T(8,128)(2,1)}), bf16[4,4,144,256]{3,2,1,0:T(8,128)(2,1)S(1)}, u32[]{:S(2)}, u32[]{:S(2)}) async-start(bf16[4,4,144,256]{3,2,1,0:T(8,128)(2,1)} %decode.1), calls=%async_computation | async-start | bytes 2359296 | tf_op jit(solution)/shard_map/all_to_all | solution.py:293
  75.2 10.3 %collective-permute-start.5 = (f32[2,256]{1,0:T(2,128)S(1)}, f32[2,256]{1,0:T(2,128)S(1)}, u32[]{:S(2)}, u32[]{:S(2)}) collective-permute-start(f32[2,256]{1,0:T(2,128)S(1)} %multiply_add_fusion.1), channel_id=1, source_target_pairs={{0,12},{4,0},{8,4},{12,8},{1,13},{5,1},{9,5},{13,9},{2,14},{6,2},{... | collective-permute-start | bytes 6152 | tf_op jit(solution)/shard_map/ppermute | solution.py:262
  79.0 15.9 %collective-permute-start.4 = (f32[2,256]{1,0:T(2,128)S(1)}, f32[2,256]{1,0:T(2,128)S(1)}, u32[]{:S(2)}, u32[]{:S(2)}) collective-permute-start(f32[2,256]{1,0:T(2,128)S(1)} %multiply_add_fusion.1), channel_id=1, source_target_pairs={{0,8},{4,12},{8,0},{12,4},{1,9},{5,13},{9,1},{13,5},{2,10},{6,14},... | collective-permute-start | bytes 6152 | tf_op jit(solution)/shard_map/ppermute | solution.py:262
  79.0 15.9 %collective-permute-start.3 = (f32[2,256]{1,0:T(2,128)S(1)}, f32[2,256]{1,0:T(2,128)S(1)}, u32[]{:S(2)}, u32[]{:S(2)}) collective-permute-start(f32[2,256]{1,0:T(2,128)S(1)} %multiply_add_fusion.1), channel_id=1, source_target_pairs={{0,4},{4,8},{8,12},{12,0},{1,5},{5,9},{9,13},{13,1},{2,6},{6,10},{... | collective-permute-start | bytes 6152 | tf_op jit(solution)/shard_map/ppermute | solution.py:262
  95.6 1.0 %copy-start.1 = (bf16[4,4,144,256]{3,2,1,0:T(8,128)(2,1)}, bf16[4,4,144,256]{3,2,1,0:T(8,128)(2,1)S(1)}, u32[]{:S(2)}) copy-start(bf16[4,4,144,256]{3,2,1,0:T(8,128)(2,1)S(1)} %all-to-all-done.part) | copy-start | bytes 3538948

commit v2 on v1

--- a/solution.py
+++ b/solution.py
@@ -17,13 +17,24 @@
 SCALE = HD ** -0.5 * math.log2(math.e)
 NN = (((1,), (0,)), ((), ()))
 EXTRA = 16
-UNROLL = 2
+UNROLL = (4, 2, 1)
 CHUNK = 512
 VMEM_LIMIT = 48 * 1024 * 1024
 
 
 def dot(a, b, dims):
     return lax.dot_general(a, b, dims, preferred_element_type=jnp.float32)
+
+
+def scaled_pieces(q_rows, q_s):
+    turned = q_rows[...].T * SCALE
+    high = turned.astype(jnp.bfloat16)
+    q_s[:HD] = high
+    q_s[HD:] = (turned - high.astype(jnp.float32)).astype(jnp.bfloat16)
+
+
+def twice(key):
+    return jnp.concatenate([key, key], axis=1)
 
 
 def decode_kernel(parts, steps, meta, keep, pick, dq, dk, dv, k_ref, v_ref, out, q_rows, q_s, acc, m_s, l_s):
@@ -38,7 +49,7 @@
     for d in range(parts):
         for g in range(group):
             q_rows[pl.ds(d * cols + g * per, per), :] = gathered[d * per:(d + 1) * per, g * HD:(g + 1) * HD]
-    q_s[...] = q_rows[...].T.astype(jnp.bfloat16)
+    scaled_pieces(q_rows, q_s)
     acc[...] = jnp.zeros_like(acc)
     m_s[...] = jnp.full_like(m_s, FILL)
     l_s[...] = jnp.zeros_like(l_s)
@@ -53,8 +64,8 @@
         at = pl.ds(d * wide, wide)
         m_old = m_s[:, at]
         m_new = jnp.maximum(m_old, jnp.max(s, axis=0, keepdims=True))
-        p = jnp.exp2(s * SCALE - m_new * SCALE)
-        shrink = jnp.exp2((m_old - m_new) * SCALE)
+        p = jnp.exp2(s - m_new)
+        shrink = jnp.exp2(m_old - m_new)
         both = dot(turned, p.astype(jnp.bfloat16), NN)
         m_s[:, at] = m_new
         l_s[:, at] = l_s[:, at] * shrink + both[HD:HD + 1]
@@ -65,7 +76,7 @@
         for key, value in blocks:
             ones = jnp.ones((EXTRA, value.shape[0]), jnp.bfloat16)
             turned = jnp.concatenate([value.T, ones], axis=0)
-            work += [(key, turned, d) for d in range(chunks)]
+            work += [(twice(key), turned, d) for d in range(chunks)]
         later = score(work[0][0], work[0][2])
         for at, (_, turned, d) in enumerate(work):
             s = later
@@ -87,16 +98,15 @@
         at = pl.ds(pl.multiple_of((keep[head, start + i] - base) * STRETCH, STRETCH), STRETCH)
         return k_ref[at, :], v_ref[at, :]
 
-    def several(i, carry):
-        update([block(i * UNROLL + u) for u in range(UNROLL)])
-        return carry
-
-    def one(i, carry):
-        update([block(i)])
-        return carry
-
-    lax.fori_loop(0, many // UNROLL, several, 0)
-    lax.fori_loop(many // UNROLL * UNROLL, many, one, 0)
+    done = 0
+    for size in UNROLL:
+        def several(i, carry, size=size, done=done):
+            update([block(done + i * size + u) for u in range(size)])
+            return carry
+
+        times = (many - done) // size
+        lax.fori_loop(0, times, several, 0)
+        done = done + times * size
 
     @pl.when(meta[1] == 1)
     def _():
@@ -104,15 +114,14 @@
         update([(k_ref[tail, :], v_ref[tail, :])])
         own_k = dot(pick[...], dk[...], NN).astype(jnp.bfloat16)
         own_v = dot(pick[...], dv[...], NN).astype(jnp.bfloat16)
-        each = per // steps
 
         def mask(d, shape):
             key_at = lax.broadcasted_iota(jnp.int32, shape, 0)
             query = lax.broadcasted_iota(jnp.int32, shape, 1) + d * wide
             query_at = query % per
             inside = key_at % per
-            return ((key_at // per == query // cols) & (inside % each == query_at % each)
-                    & (inside // each <= query_at // each))
+            return ((key_at // per == query // cols) & (inside // steps == query_at // steps)
+                    & (inside % steps <= query_at % steps))
 
         update([(own_k, own_v)], mask)
 
@@ -120,7 +129,7 @@
     some = l > 0.0
     safe = jnp.where(some, l, 1.0)
     inverse = jnp.where(some, 1.0 / safe, 0.0)
-    level = jnp.where(some, m_s[...] * SCALE + jnp.log2(safe), FILL)
+    level = jnp.where(some, m_s[...] + jnp.log2(safe), FILL)
     high = level.astype(jnp.bfloat16).astype(jnp.float32)
     middle = (level - high).astype(jnp.bfloat16).astype(jnp.float32)
     low = level - high - middle
@@ -154,7 +163,7 @@
             out_specs=pl.BlockSpec((parts, None, HD + EXTRA, cols), lambda h, *_: (0, h, 0, 0)),
             scratch_shapes=[
                 pltpu.VMEM((count, HD), jnp.float32),
-                pltpu.VMEM((HD, count), jnp.bfloat16),
+                pltpu.VMEM((2 * HD, count), jnp.bfloat16),
                 pltpu.VMEM((HD, count), jnp.float32),
                 pltpu.VMEM((1, count), jnp.float32),
                 pltpu.VMEM((1, count), jnp.float32),
@@ -174,12 +183,12 @@
     group = q_ref.shape[1] // HD
     for g in range(group):
         q_rows[pl.ds(g * W, W), :] = q_ref[:, pl.ds(g * HD, HD)].astype(jnp.float32)
-    q_s[...] = q_rows[...].T.astype(jnp.bfloat16)
+    scaled_pieces(q_rows, q_s)
     stretches = k_ref.shape[0] // STRETCH
     several = math.gcd(stretches, 4)
 
     def score(c):
-        return dot(k_ref[pl.ds(pl.multiple_of(c * STRETCH, STRETCH), STRETCH), :], q_s[...], NN)
+        return dot(twice(k_ref[pl.ds(pl.multiple_of(c * STRETCH, STRETCH), STRETCH), :]), q_s[...], NN)
 
     def levels(first, last):
         later = score(first)
@@ -192,8 +201,8 @@
                 query_at = lax.broadcasted_iota(jnp.int32, s.shape, 1) % W
                 s = jnp.where((key_at <= STRETCH - W + query_at) | (meta[1] == 0), s, FILL)
             m = jnp.max(s, axis=0, keepdims=True)
-            total = jnp.sum(jnp.exp2(s * SCALE - m * SCALE), axis=0, keepdims=True)
-            out[pl.ds(first + u, 1), :] = m * SCALE + jnp.log2(total)
+            total = jnp.sum(jnp.exp2(s - m), axis=0, keepdims=True)
+            out[pl.ds(first + u, 1), :] = m + jnp.log2(total)
 
     def one(c, carry):
         levels(c * several, False)
@@ -217,7 +226,7 @@
                 pl.BlockSpec((keys.shape[0], HD), lambda h, meta: (0, meta[2] + h)),
             ],
             out_specs=pl.BlockSpec((None, stretches, count), lambda h, meta: (h, 0, 0)),
-            scratch_shapes=[pltpu.VMEM((count, HD), jnp.float32), pltpu.VMEM((HD, count), jnp.bfloat16)],
+            scratch_shapes=[pltpu.VMEM((count, HD), jnp.float32), pltpu.VMEM((2 * HD, count), jnp.bfloat16)],
         ),
         out_shape=jax.ShapeDtypeStruct((heads, stretches, count), jnp.float32),
         compiler_params=pltpu.CompilerParams(vmem_limit_bytes=VMEM_LIMIT),
@@ -226,33 +235,34 @@
 
 
 def combine_kernel(part, out):
-    parts = part.shape[0]
-    blocks = [part[i].astype(jnp.float32) for i in range(parts)]
-    levels = [b[HD:HD + 1] + b[HD + 1:HD + 2] + b[HD + 2:HD + 3] for b in blocks]
-    top = levels[0]
-    for level in levels[1:]:
-        top = jnp.maximum(top, level)
-    total = jnp.zeros_like(top)
-    summed = jnp.zeros((HD, part.shape[2]), jnp.float32)
-    for block, level in zip(blocks, levels):
-        share = jnp.exp2(level - top)
-        total = total + share
-        summed = summed + block[:HD] * share
-    turned = (summed / total).T.astype(jnp.bfloat16)
-    per = out.shape[0]
-    for g in range(turned.shape[0] // per):
-        out[:, pl.ds(g * HD, HD)] = turned[g * per:(g + 1) * per, :]
-
-
-def combine(part, per):
-    parts, heads, depth, cols = part.shape
-    width = cols // per * HD
+    parts, heads = part.shape[:2]
+    each, steps, columns = out.shape
+    width = columns // heads
+    for h in range(heads):
+        blocks = [part[i, h].astype(jnp.float32) for i in range(parts)]
+        levels = [b[HD:HD + 1] + b[HD + 1:HD + 2] + b[HD + 2:HD + 3] for b in blocks]
+        top = functools.reduce(jnp.maximum, levels)
+        total = jnp.zeros_like(top)
+        summed = jnp.zeros((HD, part.shape[3]), jnp.float32)
+        for block, level in zip(blocks, levels):
+            share = jnp.exp2(level - top)
+            total = total + share
+            summed = summed + block[:HD] * share
+        turned = (summed / total).T
+        for g in range(width // HD):
+            rows = turned[g * each * steps:(g + 1) * each * steps]
+            out[:, :, pl.ds(h * width + g * HD, HD)] = rows.reshape(each, steps, HD).astype(jnp.bfloat16)
+
+
+def combine(part, steps, each):
+    heads, cols = part.shape[1], part.shape[3]
+    whole = pl.BlockSpec(memory_space=pltpu.VMEM)
     return pl.pallas_call(
         combine_kernel,
-        grid=(heads,),
-        in_specs=[pl.BlockSpec((parts, None, depth, cols), lambda h: (0, h, 0, 0))],
-        out_specs=pl.BlockSpec((per, width), lambda h: (0, h)),
-        out_shape=jax.ShapeDtypeStruct((per, heads * width), jnp.bfloat16),
+        in_specs=[whole],
+        out_specs=whole,
+        out_shape=jax.ShapeDtypeStruct((each, steps, heads * cols // (steps * each) * HD), jnp.bfloat16),
+        compiler_params=pltpu.CompilerParams(vmem_limit_bytes=16 * 1024 * 1024),
         name="combine",
     )(part)
 
@@ -278,7 +288,7 @@
     shifted = others(mine, "ctx")
 
     order = lax.dynamic_slice_in_dim(row_order.reshape(parts, row_count, each), row, 1, 1)
-    wanted = order * steps + jnp.arange(steps, dtype=jnp.int32)[None, :, None]
+    wanted = order.reshape(parts, each, 1) * steps + jnp.arange(steps, dtype=jnp.int32)
     pick = (wanted.reshape(-1)[:, None] == jnp.arange(rows * steps, dtype=jnp.int32)[None, :])
     pick = pick.astype(jnp.bfloat16)
 
@@ -300,8 +310,7 @@
     whole = jnp.log2(sum(jnp.exp2(one - top) for one in everyone)) + top
     stretch_scores = jnp.sum(jnp.exp2(level - whole[:, None, :]), axis=2)
 
-    decoded = combine(part, steps * each)
-    decoded = decoded.reshape(steps, each, -1).transpose(1, 0, 2)
+    decoded = combine(part, steps, each)
     return stretch_scores, decoded
 
 

time: 102 us -> 91 us (0.89)
  the two profiles are of different devices: /device:TPU:0 before, /device:TPU:6 now
where the time goes in v2:
time: 91 us; the launch traced here: 90.1 us
  Pallas kernels  52.3 us (57%)
  starting transfers between devices  14.9 us (16%)
  waiting for transfers between devices  14.9 us (16%)
  local copies, waits for them, and re-layouts  6.25 us (7%)
  other arithmetic  1 us (1%)
    pallas_call x1, Pallas kernels, decode(): pl.pallas_call(functools.partial(decode_kernel, parts, steps), grid_spec=...  43 us
    ppermute x6, waiting for transfers between devices, others(): lax.ppermute(x, axis, [(i, (i + shift) % count) for i in range(count)])  14.9 us
    ppermute x6, starting transfers between devices, others(): lax.ppermute(x, axis, [(i, (i + shift) % count) for i in range(count)])  11.4 us
    pallas_call x1, Pallas kernels, window(): pl.pallas_call(window_kernel, grid_spec=pltpu.PrefetchScalarGridSpec(num_...  8.17 us
    reshape x3, local copies, waits for them, and re-layouts, local(): flat = lambda x: x.reshape(rows * steps, x.shape[2])  4.58 us
    all_to_all x1, starting transfers between devices, local(): part = lax.all_to_all(part, 'ctx', 0, 0, tiled=True)  3.53 us
  transfers between devices with their start and end apart: 7, of which 2 were waited for; matrix products, arithmetic and copies ran while one was open for 7% of the time, Pallas kernels for 9%

profile of v2, /device:TPU:6, one launch (start us, length us, event | category | flops | bytes accessed | tf_op | source)
XLA Modules:
  0.0 90.1 jit_solution(9715481698536241001)
XLA Ops:
  0.7 0.8 constant_dynamic-update-slice_fusion.3
  1.4 2.6 %collective-permute-start.1 = (bf16[8,2048]{1,0:T(8,128)(2,1)S(1)}, bf16[8,2048]{1,0:T(8,128)(2,1)S(1)}, u32[]{:S(2)}, u32[]{:S(2)}) collective-permute-start(bf16[8,2048]{1,0:T(8,128)(2,1)S(1)} %get-tuple-element.7), channel_id=1, source_target_pairs={{0,8},{4,12},{8,0},{12,4},{1,9},{5,13},{9,1},{13,5},{2,10},{6,14},... | collective-permute-start | bytes 98312 | tf_op jit(solution)/shard_map/ppermute | solution.py:272
  4.0 1.6 %collective-permute-start = (bf16[8,2048]{1,0:T(8,128)(2,1)S(1)}, bf16[8,2048]{1,0:T(8,128)(2,1)S(1)}, u32[]{:S(2)}, u32[]{:S(2)}) collective-permute-start(bf16[8,2048]{1,0:T(8,128)(2,1)S(1)} %get-tuple-element.7), channel_id=1, source_target_pairs={{0,4},{4,8},{8,12},{12,0},{1,5},{5,9},{9,13},{13,1},{2,6},{6,10},{... | collective-permute-start | bytes 98312 | tf_op jit(solution)/shard_map/ppermute | solution.py:272
  5.6 2.2 %collective-permute-start.2 = (bf16[8,2048]{1,0:T(8,128)(2,1)S(1)}, bf16[8,2048]{1,0:T(8,128)(2,1)S(1)}, u32[]{:S(2)}, u32[]{:S(2)}) collective-permute-start(bf16[8,2048]{1,0:T(8,128)(2,1)S(1)} %get-tuple-element.7), channel_id=1, source_target_pairs={{0,12},{4,0},{8,4},{12,8},{1,13},{5,1},{9,5},{13,9},{2,14},{6,2},{... | collective-permute-start | bytes 98312 | tf_op jit(solution)/shard_map/ppermute | solution.py:272
  7.8 0.7 reshape.42
  8.6 0.1 iota_add_fusion
  8.7 0.1 add.78
  8.8 0.1 fusion.pick
  8.9 0.1 pad_add_fusion.meta
  9.0 1.0 %reshape.44.dk = bf16[256,512]{1,0:T(8,128)(2,1)S(1)} reshape(bf16[64,4,512]{2,1,0:T(4,128)(2,1)} %param.13) | data formatting | bytes 524288 | tf_op jit(solution)/shard_map/reshape | solution.py:301
  10.0 1.0 %reshape.45.dv = bf16[256,512]{1,0:T(8,128)(2,1)S(1)} reshape(bf16[64,4,512]{2,1,0:T(4,128)(2,1)} %param.14) | data formatting | bytes 524288 | tf_op jit(solution)/shard_map/reshape | solution.py:301
  11.0 0.0 copy-start
  11.0 2.5 %reshape.43.dq = bf16[256,4096]{1,0:T(8,128)(2,1)S(1)} reshape(bf16[64,4,4096]{2,1,0:T(4,128)(2,1)} %param.12) | data formatting | bytes 4194304 | tf_op jit(solution)/shard_map/reshape | solution.py:301
  13.6 0.0 collective-permute-done
  13.6 0.0 collective-permute-done.1
  13.6 0.0 collective-permute-done.2
  13.7 0.0 copy-done
  13.7 43.0 %decode.1 = bf16[4,4,144,256]{3,2,1,0:T(8,128)(2,1)} custom-call(s32[3]{0:T(128)S(1)} %pad_add_fusion.meta, s32[4,20]{1,0:T(4,128)S(1)} %copy-done, bf16[128,256]{1,0:T(8,128)(2,1)S(1)} %fusion.pick, bf16[256,4096]{1,0:T(8,128)(2,1)S(1)} %reshape.43.dq, bf16[256,512]{1,0:T(8,128)(2,1)S(1)} %reshape.44.dk, bf16[256,512]{1,0:T(8,128)(2,1)S(1)} %reshape.45.dv, ...), custom_call_target="tpu_custom_call" | custom-call | flops 8589934592 | bytes 16777216 | tf_op jit(solution)/shard_map/decode/pallas_call | solution.py:150
  56.7 3.5 %all-to-all-start = ((bf16[4,4,144,256]{3,2,1,0:T(8,128)(2,1)}), bf16[4,4,144,256]{3,2,1,0:T(8,128)(2,1)S(1)}, u32[]{:S(2)}, u32[]{:S(2)}) async-start(bf16[4,4,144,256]{3,2,1,0:T(8,128)(2,1)} %decode.1), calls=%async_computation | async-start | bytes 2359296 | tf_op jit(solution)/shard_map/all_to_all | solution.py:303
  60.3 8.2 %window.1 = f32[2,16,256]{2,1,0:T(8,128)S(1)} custom-call(s32[3]{0:T(128)S(1)} %pad_add_fusion.meta, bf16[32,2048]{1,0:T(8,128)(2,1)S(1)} %constant_dynamic-update-slice_fusion.q_ref, bf16[8192,512]{1,0:T(8,128)(2,1)} %k_ref.3), custom_call_target="tpu_custom_call" | custom-call | tf_op jit(solution)/shard_map/window/pallas_call | solution.py:219
  68.5 3.8 %collective-permute-start.5 = (f32[2,256]{1,0:T(2,128)S(1)}, f32[2,256]{1,0:T(2,128)S(1)}, u32[]{:S(2)}, u32[]{:S(2)}) collective-permute-start(f32[2,256]{1,0:T(2,128)S(1)} %multiply_add_fusion.1), channel_id=1, source_target_pairs={{0,12},{4,0},{8,4},{12,8},{1,13},{5,1},{9,5},{13,9},{2,14},{6,2},{... | collective-permute-start | bytes 6152 | tf_op jit(solution)/shard_map/ppermute | solution.py:272
  72.4 0.0 collective-permute-start.4
  72.4 1.1 %collective-permute-start.3 = (f32[2,256]{1,0:T(2,128)S(1)}, f32[2,256]{1,0:T(2,128)S(1)}, u32[]{:S(2)}, u32[]{:S(2)}) collective-permute-start(f32[2,256]{1,0:T(2,128)S(1)} %multiply_add_fusion.1), channel_id=1, source_target_pairs={{0,4},{4,8},{8,12},{12,0},{1,5},{5,9},{9,13},{13,1},{2,6},{6,10},{... | collective-permute-start | bytes 6152 | tf_op jit(solution)/shard_map/ppermute | solution.py:272
  73.5 5.5 %collective-permute-done.5 = f32[2,256]{1,0:T(2,128)S(1)} collective-permute-done((f32[2,256]{1,0:T(2,128)S(1)}, f32[2,256]{1,0:T(2,128)S(1)}, u32[]{:S(2)}, u32[]{:S(2)}) %collective-permute-start.5) | collective-permute-done | bytes 2080 | tf_op jit(solution)/shard_map/ppermute | solution.py:272
  79.0 9.4 %collective-permute-done.4 = f32[2,256]{1,0:T(2,128)S(1)} collective-permute-done((f32[2,256]{1,0:T(2,128)S(1)}, f32[2,256]{1,0:T(2,128)S(1)}, u32[]{:S(2)}, u32[]{:S(2)}) %collective-permute-start.4) | collective-permute-done | bytes 2080 | tf_op jit(solution)/shard_map/ppermute | solution.py:272
  88.4 0.0 collective-permute-done.3
  88.4 0.7 exponential_reduce_fusion
  89.1 0.0 all-to-all-done.part
  89.1 1.1 %combine.1 = bf16[8,4,4096]{2,1,0:T(4,128)(2,1)} custom-call(bf16[4,4,144,256]{3,2,1,0:T(8,128)(2,1)S(1)} %all-to-all-done.part), custom_call_target="tpu_custom_call" | custom-call | tf_op jit(solution)/shard_map/combine/pallas_call | solution.py:260
  (9 shorter events, 0.1 us)
Async XLA Ops:
  1.4 12.2 %collective-permute-start.1 = (bf16[8,2048]{1,0:T(8,128)(2,1)S(1)}, bf16[8,2048]{1,0:T(8,128)(2,1)S(1)}, u32[]{:S(2)}, u32[]{:S(2)}) collective-permute-start(bf16[8,2048]{1,0:T(8,128)(2,1)S(1)} %get-tuple-element.7), channel_id=1, source_target_pairs={{0,8},{4,12},{8,0},{12,4},{1,9},{5,13},{9,1},{13,5},{2,10},{6,14},... | collective-permute-start | bytes 98312 | tf_op jit(solution)/shard_map/ppermute | solution.py:272
  4.0 9.6 %collective-permute-start = (bf16[8,2048]{1,0:T(8,128)(2,1)S(1)}, bf16[8,2048]{1,0:T(8,128)(2,1)S(1)}, u32[]{:S(2)}, u32[]{:S(2)}) collective-permute-start(bf16[8,2048]{1,0:T(8,128)(2,1)S(1)} %get-tuple-element.7), channel_id=1, source_target_pairs={{0,4},{4,8},{8,12},{12,0},{1,5},{5,9},{9,13},{13,1},{2,6},{6,10},{... | collective-permute-start | bytes 98312 | tf_op jit(solution)/shard_map/ppermute | solution.py:272
  5.6 8.0 %collective-permute-start.2 = (bf16[8,2048]{1,0:T(8,128)(2,1)S(1)}, bf16[8,2048]{1,0:T(8,128)(2,1)S(1)}, u32[]{:S(2)}, u32[]{:S(2)}) collective-permute-start(bf16[8,2048]{1,0:T(8,128)(2,1)S(1)} %get-tuple-element.7), channel_id=1, source_target_pairs={{0,12},{4,0},{8,4},{12,8},{1,13},{5,1},{9,5},{13,9},{2,14},{6,2},{... | collective-permute-start | bytes 98312 | tf_op jit(solution)/shard_map/ppermute | solution.py:272
  11.0 2.7 %copy-start = (s32[4,20]{1,0:T(4,128)S(1)}, s32[4,20]{1,0:T(4,128)}, u32[]{:S(2)}) copy-start(s32[4,20]{1,0:T(4,128)} %keep.1) | copy-start | bytes 964
  56.7 32.3 %all-to-all-start = ((bf16[4,4,144,256]{3,2,1,0:T(8,128)(2,1)}), bf16[4,4,144,256]{3,2,1,0:T(8,128)(2,1)S(1)}, u32[]{:S(2)}, u32[]{:S(2)}) async-start(bf16[4,4,144,256]{3,2,1,0:T(8,128)(2,1)} %decode.1), calls=%async_computation | async-start | bytes 2359296 | tf_op jit(solution)/shard_map/all_to_all | solution.py:303
  68.5 10.5 %collective-permute-start.5 = (f32[2,256]{1,0:T(2,128)S(1)}, f32[2,256]{1,0:T(2,128)S(1)}, u32[]{:S(2)}, u32[]{:S(2)}) collective-permute-start(f32[2,256]{1,0:T(2,128)S(1)} %multiply_add_fusion.1), channel_id=1, source_target_pairs={{0,12},{4,0},{8,4},{12,8},{1,13},{5,1},{9,5},{13,9},{2,14},{6,2},{... | collective-permute-start | bytes 6152 | tf_op jit(solution)/shard_map/ppermute | solution.py:272
  72.4 16.0 %collective-permute-start.4 = (f32[2,256]{1,0:T(2,128)S(1)}, f32[2,256]{1,0:T(2,128)S(1)}, u32[]{:S(2)}, u32[]{:S(2)}) collective-permute-start(f32[2,256]{1,0:T(2,128)S(1)} %multiply_add_fusion.1), channel_id=1, source_target_pairs={{0,8},{4,12},{8,0},{12,4},{1,9},{5,13},{9,1},{13,5},{2,10},{6,14},... | collective-permute-start | bytes 6152 | tf_op jit(solution)/shard_map/ppermute | solution.py:272
  72.4 16.0 %collective-permute-start.3 = (f32[2,256]{1,0:T(2,128)S(1)}, f32[2,256]{1,0:T(2,128)S(1)}, u32[]{:S(2)}, u32[]{:S(2)}) collective-permute-start(f32[2,256]{1,0:T(2,128)S(1)} %multiply_add_fusion.1), channel_id=1, source_target_pairs={{0,4},{4,8},{8,12},{12,0},{1,5},{5,9},{9,13},{13,1},{2,6},{6,10},{... | collective-permute-start | bytes 6152 | tf_op jit(solution)/shard_map/ppermute | solution.py:272
